TPU v7x, 32 devices: a whole 2x2x4 slice. The times are simulated.
32 devices in a mesh: dp: 16 (over z, y, x), mp: 2 (over core).
Axes of the slice: x: 2, y: 2, z: 4, core: 2. Of those that a mesh axis runs over, the one named last changes fastest.
Arguments:
- layer_input: bfloat16 [16, 512, 512], P('dp'), may hold values from -6 to 6
- memory: bfloat16 [2, 16, 512, 512], P(None, 'dp'), may hold values from -6 to 6
- doc_lengths: int32 [16, 4], P('dp'), may hold values from 1 to 256, 448 in all within a row
- neighbour_owner: int32 [16, 512, 4], P('dp'), may hold values from 0 to 15, all different within a row; in each aligned block of 512 rows (0 to 511, 512 to 1023, ..., all dimensions but the last counted through in order) at most 256 rows name the same one
- neighbour_row: int32 [16, 512, 4], P('dp'), may hold values from 0 to 1023
- table: bfloat16 [16384, 512], P('dp'), may hold values from -6 to 6
- gain_attn: float32 [2, 512], replicated, may hold values from 0.5 to 1.5
- w_query: bfloat16 [2, 512, 512], P(None, None, 'mp'), may hold values from -0.25 to 0.25
- w_key: bfloat16 [2, 512, 512], P(None, None, 'mp'), may hold values from -0.25 to 0.25
- w_value: bfloat16 [2, 512, 512], P(None, None, 'mp'), may hold values from -0.25 to 0.25
- w_out: bfloat16 [2, 512, 512], P(None, 'mp'), may hold values from -1.5 to 1.5
- gain_ffn: float32 [2, 512], replicated, may hold values from 0.5 to 1.5
- w_up: bfloat16 [2, 512, 2048], P(None, None, 'mp'), may hold values from -0.25 to 0.25
- w_down: bfloat16 [2, 2048, 512], P(None, 'mp'), may hold values from -0.125 to 0.125
- w_gate: float32 [512], replicated, may hold values from -0.25 to 0.25
- cotangent: bfloat16 [16, 512, 512], P('dp'), may hold values from -6 to 6
Outputs:
- layer_output: float32 [16, 512, 512], P('dp')
- input_grad: float32 [16, 512, 512], P('dp')
- memory_grad: float32 [2, 16, 512, 512], P(None, 'dp')
- grad_gain_attn: float32 [2, 512], replicated
- grad_w_query: float32 [2, 512, 512], P(None, None, 'mp')
- grad_w_key: float32 [2, 512, 512], P(None, None, 'mp')
- grad_w_value: float32 [2, 512, 512], P(None, None, 'mp')
- grad_w_out: float32 [2, 512, 512], P(None, 'mp')
- grad_gain_ffn: float32 [2, 512], replicated
- grad_w_up: float32 [2, 512, 2048], P(None, None, 'mp')
- grad_w_down: float32 [2, 2048, 512], P(None, 'mp')
- grad_w_gate: float32 [512], replicated
Inputs may be any that keep to these rules, and one draw needn't show every extreme that they name: `doc_lengths`: the 4 lengths of a row sum to 448; the longest is 256. `neighbour_owner`: A token's 4 owners differ. Among the tokens of one index of dp, no owner is named by more than 256 tokens, a bound that some block reaches.
All inputs are finite; a program needn't handle non-finite values.
Results may differ from a plain program's by a relative error of at most 0.024.
Values may be sent and summed in bfloat16 or wider, within the bound.
No kernel may reach another device: no remote copies, remote signals or barrier semaphores. Data moves between devices by JAX's collectives and lax.ppermute only.
A program may use at most 192 MiB of HBM per device.

v0:
```python
import math

import jax
import jax.numpy as jnp
from jax import lax
from jax.sharding import PartitionSpec as P

D = 512
HD = 64
SEG = 512
MEM = 512
LAYERS = 2


norm_eps = 1e-05


def layer_norm(values, gain_vector):
    average = jnp.mean(values, axis=-1, keepdims=True)
    centred = values - average
    inverse = lax.rsqrt(jnp.mean(centred * centred, axis=-1, keepdims=True) + norm_eps)
    return centred * inverse * gain_vector


def document_ids(doc_lengths):
    doc_ends = jnp.cumsum(doc_lengths, axis=-1)
    places = jnp.arange(SEG, dtype=jnp.int32)
    return jnp.sum((places[:, None] >= doc_ends[..., None, :]).astype(jnp.int32), axis=-1)


def allowed_keys(doc_ids):
    places = jnp.arange(doc_ids.shape[-1], dtype=jnp.int32)
    with_memory = jnp.broadcast_to((doc_ids == 0)[..., None], doc_ids.shape + (MEM,))
    same_doc = (doc_ids[..., :, None] == doc_ids[..., None, :]) & (
        places[:, None] >= places[None, :]
    )
    return jnp.concatenate([with_memory, same_doc], axis=-1)


def heads_view(values):
    return values.reshape(values.shape[0], values.shape[1], -1, HD)


def flat_heads(values):
    return values.reshape(values.shape[0], values.shape[1], -1)


def project(normed_low, w_query, w_key, w_value):
    queries = jnp.einsum(
        "rtd,de->rte", normed_low[:, MEM:], w_query, preferred_element_type=jnp.float32
    ).astype(jnp.bfloat16)
    key_rows = jnp.einsum(
        "rtd,de->rte", normed_low, w_key, preferred_element_type=jnp.float32
    ).astype(jnp.bfloat16)
    value_rows = jnp.einsum(
        "rtd,de->rte", normed_low, w_value, preferred_element_type=jnp.float32
    ).astype(jnp.bfloat16)
    return (heads_view(queries), heads_view(key_rows), heads_view(value_rows))


def raw_scores(queries, key_rows, allowed):
    score_scale = 1.0 / math.sqrt(HD)
    scores = (
        jnp.einsum("rqhd,rkhd->rhqk", queries, key_rows, preferred_element_type=jnp.float32)
        * score_scale
    )
    return jnp.where(allowed[:, None], scores, -1e30)


def attend_values(probs_low, value_rows):
    head_mixed = jnp.einsum(
        "rhqk,rkhd->rqhd", probs_low, value_rows, preferred_element_type=jnp.float32
    )
    return flat_heads(head_mixed).astype(jnp.bfloat16)


def across_cores(values):
    return lax.psum(values, "mp")


def layer_forward(hidden, memory_rows, allowed, weights):
    gain_attn, w_query, w_key, w_value, w_out, gain_ffn, w_up, w_down = weights
    full_rows = jnp.concatenate([memory_rows, hidden], axis=1)
    normed_low = layer_norm(full_rows, gain_attn).astype(jnp.bfloat16)
    queries, key_rows, value_rows = project(normed_low, w_query, w_key, w_value)
    scores = raw_scores(queries, key_rows, allowed)
    top_score = jnp.max(scores, axis=-1, keepdims=True)
    exp_scores = jnp.exp(scores - top_score)
    row_total = jnp.sum(exp_scores, axis=-1, keepdims=True)
    log_total = top_score + jnp.log(row_total)
    head_mixed = attend_values((exp_scores / row_total).astype(jnp.bfloat16), value_rows)
    attn_part = jnp.einsum("rte,ed->rtd", head_mixed, w_out, preferred_element_type=jnp.float32)
    middle = hidden + across_cores(attn_part)
    normed_ffn = layer_norm(middle, gain_ffn).astype(jnp.bfloat16)
    pre_act = jnp.einsum("rtd,df->rtf", normed_ffn, w_up, preferred_element_type=jnp.float32)
    act_low = jax.nn.gelu(pre_act).astype(jnp.bfloat16)
    ffn_part = jnp.einsum("rtf,fd->rtd", act_low, w_down, preferred_element_type=jnp.float32)
    return (middle + across_cores(ffn_part), middle, log_total)


def layer_backward(grad_out, hidden, middle, log_total, memory_rows, allowed, weights):
    gain_attn, w_query, w_key, w_value, w_out, gain_ffn, w_up, w_down = weights
    score_scale = 1.0 / math.sqrt(HD)
    normed_ffn, ffn_norm_back = jax.vjp(layer_norm, middle, gain_ffn)
    ffn_low = normed_ffn.astype(jnp.bfloat16)
    pre_act = jnp.einsum("rtd,df->rtf", ffn_low, w_up, preferred_element_type=jnp.float32)
    act_value, gelu_back = jax.vjp(jax.nn.gelu, pre_act)
    act_low = act_value.astype(jnp.bfloat16)
    grad_low = grad_out.astype(jnp.bfloat16)
    grad_down = jnp.einsum("rtf,rtd->fd", act_low, grad_low, preferred_element_type=jnp.float32)
    grad_act = jnp.einsum("rtd,fd->rtf", grad_low, w_down, preferred_element_type=jnp.float32)
    grad_pre = gelu_back(grad_act)[0].astype(jnp.bfloat16)
    grad_up = jnp.einsum("rtd,rtf->df", ffn_low, grad_pre, preferred_element_type=jnp.float32)
    grad_normed = lax.psum(
        jnp.einsum("rtf,df->rtd", grad_pre, w_up, preferred_element_type=jnp.float32), "mp"
    )
    grad_middle_norm, grad_gain_ffn = ffn_norm_back(grad_normed)
    grad_middle = grad_out + grad_middle_norm
    full_rows = jnp.concatenate([memory_rows, hidden], axis=1)
    normed_attn, attn_norm_back = jax.vjp(layer_norm, full_rows, gain_attn)
    normed_low = normed_attn.astype(jnp.bfloat16)
    queries, key_rows, value_rows = project(normed_low, w_query, w_key, w_value)
    attn_probs = jnp.exp(raw_scores(queries, key_rows, allowed) - log_total)
    probs_low = attn_probs.astype(jnp.bfloat16)
    head_mixed = attend_values(probs_low, value_rows)
    grad_branch = grad_middle.astype(jnp.bfloat16)
    grad_out_weight = jnp.einsum(
        "rte,rtd->ed", head_mixed, grad_branch, preferred_element_type=jnp.float32
    )
    grad_mixed = heads_view(
        jnp.einsum("rtd,ed->rte", grad_branch, w_out, preferred_element_type=jnp.float32).astype(
            jnp.bfloat16
        )
    )
    grad_probs = jnp.einsum(
        "rqhd,rkhd->rhqk", grad_mixed, value_rows, preferred_element_type=jnp.float32
    )
    grad_value = flat_heads(
        jnp.einsum(
            "rhqk,rqhd->rkhd", probs_low, grad_mixed, preferred_element_type=jnp.float32
        ).astype(jnp.bfloat16)
    )
    row_inner = jnp.sum(attn_probs * grad_probs, axis=-1, keepdims=True)
    grad_scores = (attn_probs * (grad_probs - row_inner)).astype(jnp.bfloat16)
    grad_query = flat_heads(
        (
            jnp.einsum("rhqk,rkhd->rqhd", grad_scores, key_rows, preferred_element_type=jnp.float32)
            * score_scale
        ).astype(jnp.bfloat16)
    )
    grad_key = flat_heads(
        (
            jnp.einsum("rhqk,rqhd->rkhd", grad_scores, queries, preferred_element_type=jnp.float32)
            * score_scale
        ).astype(jnp.bfloat16)
    )
    grad_wq = jnp.einsum(
        "rtd,rte->de", normed_low[:, MEM:], grad_query, preferred_element_type=jnp.float32
    )
    grad_wk = jnp.einsum("rtd,rte->de", normed_low, grad_key, preferred_element_type=jnp.float32)
    grad_wv = jnp.einsum("rtd,rte->de", normed_low, grad_value, preferred_element_type=jnp.float32)
    from_keys = jnp.einsum(
        "rte,de->rtd", grad_key, w_key, preferred_element_type=jnp.float32
    ) + jnp.einsum("rte,de->rtd", grad_value, w_value, preferred_element_type=jnp.float32)
    from_query = jnp.einsum("rte,de->rtd", grad_query, w_query, preferred_element_type=jnp.float32)
    from_query = jnp.concatenate([jnp.zeros_like(from_keys[:, :MEM]), from_query], axis=1)
    grad_normed_attn = lax.psum(from_keys + from_query, "mp")
    grad_full, grad_gain_attn = attn_norm_back(grad_normed_attn)
    grad_hidden = grad_middle + grad_full[:, MEM:]
    level_grads = (
        grad_gain_attn,
        grad_wq,
        grad_wk,
        grad_wv,
        grad_out_weight,
        grad_gain_ffn,
        grad_up,
        grad_down,
    )
    return (grad_hidden, grad_full[:, :MEM], level_grads)


def fetch_neighbours(neighbour_owner, neighbour_row, table):
    owners = lax.axis_size("dp")
    capacity = max(2, 2 * neighbour_owner.size // owners)
    flat_owner = neighbour_owner.reshape(-1)
    flat_row = neighbour_row.reshape(-1)
    owner_hits = (flat_owner[:, None] == jnp.arange(owners, dtype=jnp.int32)[None, :]).astype(
        jnp.int32
    )
    slot_rank = jnp.sum((jnp.cumsum(owner_hits, axis=0) - owner_hits) * owner_hits, axis=1)
    requests = jnp.zeros((owners, capacity), jnp.int32).at[flat_owner, slot_rank].set(flat_row)
    fetched = lax.all_to_all(
        jnp.take(
            table, lax.all_to_all(requests, "dp", split_axis=0, concat_axis=0, tiled=True), axis=0
        ),
        "dp",
        split_axis=0,
        concat_axis=0,
        tiled=True,
    )
    return fetched[flat_owner, slot_rank].reshape(neighbour_owner.shape + (table.shape[1],))


def retrieve(top_rows, gate_vector, neighbours):
    near_score = jnp.einsum(
        "...td,...tkd->...tk", top_rows, neighbours, precision=lax.Precision.HIGHEST
    ) / math.sqrt(D)
    near_weight = jax.nn.softmax(near_score, axis=-1)
    pooled = jnp.einsum(
        "...tk,...tkd->...td", near_weight, neighbours, precision=lax.Precision.HIGHEST
    )
    gate_value = jax.nn.sigmoid(jnp.sum(top_rows * gate_vector, axis=-1, keepdims=True))
    return top_rows + gate_value * (pooled - top_rows)


def local(
    layer_input,
    memory,
    doc_lengths,
    neighbour_owner,
    neighbour_row,
    table,
    gain_attn,
    w_query,
    w_key,
    w_value,
    w_out,
    gain_ffn,
    w_up,
    w_down,
    w_gate,
    cotangent,
):
    allowed = allowed_keys(document_ids(doc_lengths))
    stacks = (gain_attn, w_query, w_key, w_value, w_out, gain_ffn, w_up, w_down)
    hidden = layer_input.astype(jnp.float32)
    kept_rows = []
    for layer_index in range(LAYERS):
        weights = tuple((weight_stack[layer_index] for weight_stack in stacks))
        next_hidden, middle, log_total = layer_forward(
            hidden, memory[layer_index].astype(jnp.float32), allowed, weights
        )
        kept_rows.append((hidden, middle, log_total))
        hidden = next_hidden
    neighbours = fetch_neighbours(neighbour_owner, neighbour_row, table)
    neighbour_rows = neighbours.astype(jnp.float32)

    def retrieval_step(top_rows, gate_vector):
        return retrieve(top_rows, gate_vector, neighbour_rows)

    final_rows, retrieval_back = jax.vjp(retrieval_step, hidden, w_gate)
    grad_rows, grad_gate = retrieval_back(cotangent.astype(jnp.float32))
    per_level = [None] * LAYERS
    memory_grads = [None] * LAYERS
    for layer_index in range(LAYERS - 1, -1, -1):
        hidden_in, middle, log_total = kept_rows[layer_index]
        weights = tuple((weight_stack[layer_index] for weight_stack in stacks))
        grad_rows, grad_memory, level_grads = layer_backward(
            grad_rows,
            hidden_in,
            middle,
            log_total,
            memory[layer_index].astype(jnp.float32),
            allowed,
            weights,
        )
        memory_grads[layer_index] = grad_memory
        per_level[layer_index] = level_grads
    stacked = tuple((jnp.stack(grad_parts) for grad_parts in zip(*per_level)))
    summed = lax.psum(stacked + (grad_gate,), "dp")
    stacked = summed[:-1]
    gate_total = summed[-1]
    return (
        final_rows,
        grad_rows,
        jnp.stack(memory_grads),
        stacked[0],
        stacked[1],
        stacked[2],
        stacked[3],
        stacked[4],
        stacked[5],
        stacked[6],
        stacked[7],
        gate_total,
    )


def solution(mesh):
    return jax.shard_map(
        local,
        mesh=mesh,
        in_specs=(
            P("dp", None, None),
            P(None, "dp", None, None),
            P("dp", None),
            P("dp", None, None),
            P("dp", None, None),
            P("dp", None),
            P(),
            P(None, None, "mp"),
            P(None, None, "mp"),
            P(None, None, "mp"),
            P(None, "mp", None),
            P(),
            P(None, None, "mp"),
            P(None, "mp", None),
            P(),
            P("dp", None, None),
        ),
        out_specs=(
            P("dp", None, None),
            P("dp", None, None),
            P(None, "dp", None, None),
            P(),
            P(None, None, "mp"),
            P(None, None, "mp"),
            P(None, None, "mp"),
            P(None, "mp", None),
            P(),
            P(None, None, "mp"),
            P(None, "mp", None),
            P(),
        ),
        check_vma=False,
    )
```

profile of v0, /device:TPU:0, one launch (start us, length us, event | category | flops | bytes accessed | tf_op | source)
XLA Modules:
  0.0 791.3 jit_solution(1227175962521028350)
XLA Ops:
  8.5 2.7 convert_bitcast_fusion
  26.2 4.5 reduce-window.6
  32.2 8.6 %scatter_custom_fusion = s32[4096]{0:T(1024)} fusion(s32[2048]{0:T(1024)S(1)} %broadcast_select_fusion.1, s32[2048]{0:T(1024)S(1)} %reshape.1821, s32[]{:T(128)} %constant.36.clone.1), kind=kCustom, calls=%fused_computation.263 | custom fusion | bytes 16388
  40.8 8.3 %all-to-all-start = ((s32[16,1,256]{2,1,0:T(1,128)}), s32[16,1,256]{2,1,0:T(1,128)S(1)}, u32[]{:S(2)}, u32[]{:S(2)}) async-start(s32[16,1,256]{2,1,0:T(1,128)} %bitcast.48), calls=%async_computation | async-start | bytes 32768 | tf_op jit(solution)/shard_map/all_to_all | solution.py:195
  56.5 17.3 %gather_fusion = bf16[4096,512]{1,0:T(8,128)(2,1)} fusion(bf16[1024,512]{1,0:T(8,128)(2,1)S(1)} %copy-done, s32[4096]{0:T(1024)S(1)} %broadcast_clamp_fusion), kind=kCustom, calls=%fused_computation | custom fusion | bytes 8404992 | tf_op jit(solution)/shard_map/jit(_take)/gather | solution.py:194
  73.8 4.1 broadcast_select_fusion
  77.9 6.0 all-to-all-start.1
  99.0 20.9 %all-reduce.18.cloned.1.call-done = f32[1,512,512]{2,1,0:T(8,128)} async-done(((f32[1,512,512]{2,1,0:T(8,128)}), f32[1,512,512]{2,1,0:T(8,128)}) %all-reduce.18.cloned.1.call-update) | async-done | bytes 1048592 | tf_op jit(solution)/shard_map/psum | solution.py:78
  125.8 20.9 %all-reduce.20.cloned.1.call-done = f32[1,512,512]{2,1,0:T(8,128)} async-done(((f32[1,512,512]{2,1,0:T(8,128)}), f32[1,512,512]{2,1,0:T(8,128)}) %all-reduce.20.cloned.1.call-update) | async-done | bytes 1048592 | tf_op jit(solution)/shard_map/psum | solution.py:78
  149.1 13.5 %all-to-all-done.1 = bf16[16,256,512]{2,1,0:T(8,128)(2,1)} async-done(((bf16[16,256,512]{2,1,0:T(8,128)(2,1)}), bf16[16,256,512]{2,1,0:T(8,128)(2,1)}, u32[]{:S(2)}, u32[]{:S(2)}) %all-to-all-start.1) | async-done | bytes 4194336 | tf_op jit(solution)/shard_map/all_to_all | solution.py:193
  162.6 37.0 %gather_fusion.1 = bf16[2048,512]{1,0:T(8,128)(2,1)} fusion(bf16[16,256,512]{2,1,0:T(8,128)(2,1)} %all-to-all-done.1, s32[2048]{0:T(1024)S(1)} %bitcast.371), kind=kCustom, calls=%fused_computation.1 | custom fusion | bytes 4210688 | tf_op jit(solution)/shard_map/gather | solution.py:202
  199.6 4.1 reshape.1784
  203.7 10.4 %fusion.66 = f32[512,1,4]{2,1,0:T(1,128)} fusion(bf16[512,4,512]{2,1,0:T(4,128)(2,1)} %reshape.1784, f32[512,512,1]{1,0,2:T(8,128)} %bitcast.374), kind=kOutput, calls=%fused_computation.172 | convolution fusion | flops 12582912 | bytes 3153920 | tf_op jit(solution)/shard_map/jvp(...td,...tkd->...tk)/dot_general | solution.py:206
  216.1 5.4 fusion.167
  223.6 8.3 %fusion.64 = f32[512,1,4]{2,1,0:T(1,128)} fusion(bf16[512,4,512]{2,1,0:T(4,128)(2,1)S(1)} %copy-done.78, f32[512,512,1]{1,0,2:T(8,128)S(1)} %fusion.32), kind=kOutput, calls=%fused_computation.170 | convolution fusion | flops 12582912 | bytes 3153920 | tf_op jit(solution)/shard_map/transpose(jvp(...tk,...tkd->...td))/dot_general | solution.py:210
  233.8 5.4 fusion.168
  244.3 33.6 %all-reduce.22.cloned.1.call-done = f32[1,512,512]{2,1,0:T(8,128)} async-done(((f32[1,512,512]{2,1,0:T(8,128)}), f32[1,512,512]{2,1,0:T(8,128)}) %all-reduce.22.cloned.1.call-update) | async-done | bytes 1048592 | tf_op jit(solution)/shard_map/psum | solution.py:114
  283.8 5.0 convolution_convert_fusion.5
  288.9 2.7 multiply_reduce_fusion.1
  299.3 5.8 convolution_convert_fusion.11
  305.1 6.3 convolution_convert_fusion.10
  311.4 10.4 %all-reduce.24.cloned.1.call-done = f32[1,1024,512]{2,1,0:T(8,128)} async-done(((f32[1,1024,512]{2,1,0:T(8,128)}), f32[1,1024,512]{2,1,0:T(8,128)}) %all-reduce.24.cloned.1.call-update) | async-done | bytes 2097168 | tf_op jit(solution)/shard_map/psum | solution.py:167
  321.8 3.4 multiply_reduce_fusion.2
  335.4 4.6 convolution_bitcast_fusion
  347.1 8.9 %all-reduce.26.cloned.1.call-done = f32[1,512,512]{2,1,0:T(8,128)} async-done(((f32[1,512,512]{2,1,0:T(8,128)}), f32[1,512,512]{2,1,0:T(8,128)}) %all-reduce.26.cloned.1.call-update) | async-done | bytes 1048592 | tf_op jit(solution)/shard_map/psum | solution.py:114
  361.4 5.0 convolution_convert_fusion.4
  377.7 2.7 convolution_bitcast_fusion.1
  393.4 5.8 all-reduce.28.cloned.1.call-done
  399.2 2.9 multiply_reduce_fusion.3
  402.2 80.8 %all-reduce.2 = (f32[2,512]{1,0:T(2,128)}, f32[2,512]{1,0:T(2,128)}, f32[512]{0:T(512)}) all-reduce(f32[2,512]{1,0:T(2,128)S(1)} %get-tuple-element.69, f32[2,512]{1,0:T(2,128)S(1)} %get-tuple-element.70, f32[512]{0:T(512)S(1)} %get-tuple-element.43), channel_id=1, replica_groups=mesh['dp'=16,'mp'=2] {'dp'}, use_global_device_ids=true, to_apply=%region_43.44 | all-reduce | flops 2560 | bytes 20480 | tf_op jit(solution)/shard_map/psum | solution.py:271
  483.0 2.6 fusion.155
  489.8 283.3 %all-reduce.30.cloned.1.call-done = (f32[2,512,256]{2,1,0:T(8,128)}, f32[2,512,256]{2,1,0:T(8,128)}, f32[2,512,256]{2,1,0:T(8,128)}, f32[2,256,512]{2,1,0:T(8,12...) async-done(((f32[2,512,256]{2,1,0:T(8,128)}, f32[2,512,256]{2,1,0:T(8,128)}, f32[2,512,256]{2,1,0:T(8,128)}, f32[2,256,512]{2,1,0:T(8,128)}, ...) | async-done | bytes 12582928 | tf_op jit(solution)/shard_map/psum | solution.py:271
  (433 shorter events, 133.9 us)
Async XLA Ops:
  7.2 49.3 %copy-start = (bf16[1024,512]{1,0:T(8,128)(2,1)S(1)}, bf16[1024,512]{1,0:T(8,128)(2,1)}, u32[]{:S(2)}) copy-start(bf16[1024,512]{1,0:T(8,128)(2,1)} %param.21) | copy-start | bytes 3145732
  7.2 42.2 %all-reduce.14.cloned.1.call-start = ((), (), s32[]{:S(2)}) async-start(), calls=%async_computation.2 | async-start | bytes 2097152 | tf_op jit(solution)/shard_map/psum | solution.py:78
  11.2 75.9 %copy-start.6 = (f32[1,512,512]{2,1,0:T(8,128)}, f32[1,512,512]{2,1,0:T(8,128)S(1)}, u32[]{:S(2)}) copy-start(f32[1,512,512]{2,1,0:T(8,128)S(1)} %get-tuple-element.45) | copy-start | bytes 3145732
  24.2 7.3 copy-start.120
  25.5 6.4 copy-start.124
  25.5 6.5 copy-start.123
  25.5 23.8 %copy-start.122 = (f32[2,512]{1,0:T(2,128)S(1)}, f32[2,512]{1,0:T(2,128)}, u32[]{:S(2)}) copy-start(f32[2,512]{1,0:T(2,128)} %param.27) | copy-start | bytes 12292
  40.8 15.7 %all-to-all-start = ((s32[16,1,256]{2,1,0:T(1,128)}), s32[16,1,256]{2,1,0:T(1,128)S(1)}, u32[]{:S(2)}, u32[]{:S(2)}) async-start(s32[16,1,256]{2,1,0:T(1,128)} %bitcast.48), calls=%async_computation | async-start | bytes 32768 | tf_op jit(solution)/shard_map/all_to_all | solution.py:195
  49.1 34.9 %all-reduce.16.cloned.1.call-start = ((), (), s32[]{:S(2)}) async-start(), calls=%async_computation.3 | async-start | bytes 2097152 | tf_op jit(solution)/shard_map/psum | solution.py:78
  77.9 84.7 %all-to-all-start.1 = ((bf16[16,256,512]{2,1,0:T(8,128)(2,1)}), bf16[16,256,512]{2,1,0:T(8,128)(2,1)}, u32[]{:S(2)}, u32[]{:S(2)}) async-start(bf16[16,256,512]{2,1,0:T(8,128)(2,1)} %broadcast_select_fusion), calls=%async_computation.1 | async-start | bytes 8388608 | tf_op jit(solution)/shard_map/all_to_all | solution.py:193
  83.9 36.0 %all-reduce.18.cloned.1.call-start = ((), (), s32[]{:S(2)}) async-start(), calls=%async_computation.4 | async-start | bytes 2097152 | tf_op jit(solution)/shard_map/psum | solution.py:78
  99.0 47.8 %all-reduce.20.cloned.1.call-start = ((), (), s32[]{:S(2)}) async-start(), calls=%async_computation.5 | async-start | bytes 2097152 | tf_op jit(solution)/shard_map/psum | solution.py:78
  125.8 152.1 %all-reduce.22.cloned.1.call-start = ((), (), s32[]{:S(2)}) async-start(), calls=%async_computation.6 | async-start | bytes 2097152 | tf_op jit(solution)/shard_map/psum | solution.py:114
  216.1 5.4 copy-start.39
  216.1 5.4 copy-start.118
  233.8 5.5 copy-start.40
  233.8 5.5 copy-start.77
  233.8 5.5 copy-start.127
  244.2 77.6 %all-reduce.24.cloned.1.call-start = ((), (), s32[]{:S(2)}) async-start(), calls=%async_computation.7 | async-start | bytes 4194304 | tf_op jit(solution)/shard_map/psum | solution.py:167
  281.4 7.5 slice-start.2
  288.9 8.5 %copy-start.48 = (bf16[4,64,1024]{2,1,0:T(8,128)(2,1)}, bf16[4,64,1024]{2,1,0:T(8,128)(2,1)S(1)}, u32[]{:S(2)}) copy-start(bf16[4,64,1024]{2,1,0:T(8,128)(2,1)S(1)} %convolution_convert_fusion.5) | copy-start | bytes 1572868
  299.3 56.8 %all-reduce.26.cloned.1.call-start = ((), (), s32[]{:S(2)}) async-start(), calls=%async_computation.8 | async-start | bytes 2097152 | tf_op jit(solution)/shard_map/psum | solution.py:114
  299.3 5.8 copy-start.47
  335.1 64.1 %all-reduce.28.cloned.1.call-start = ((), (), s32[]{:S(2)}) async-start(), calls=%async_computation.9 | async-start | bytes 4194304 | tf_op jit(solution)/shard_map/psum | solution.py:167
  359.7 6.7 slice-start
  366.4 8.3 %copy-start.50 = (bf16[4,64,1024]{2,1,0:T(8,128)(2,1)}, bf16[4,64,1024]{2,1,0:T(8,128)(2,1)S(1)}, u32[]{:S(2)}) copy-start(bf16[4,64,1024]{2,1,0:T(8,128)(2,1)S(1)} %convolution_convert_fusion.4) | copy-start | bytes 1572868
  376.7 396.4 %all-reduce.30.cloned.1.call-start = ((), (), s32[]{:S(2)}) async-start(), calls=%async_computation.10 | async-start | bytes 25165824 | tf_op jit(solution)/shard_map/psum | solution.py:271
  393.4 5.8 copy-start.5
  393.4 5.8 copy-start.9
  393.4 5.8 copy-start.111
  393.4 89.5 %copy-start.117 = (f32[1024]{0:T(1024)S(1)}, f32[1024]{0:T(1024)}, u32[]{:S(2)}) copy-start(f32[1024]{0:T(1024)} %copy-done.116) | copy-start | bytes 12292
  393.4 89.5 %copy-start.113 = (f32[1024]{0:T(1024)S(1)}, f32[1024]{0:T(1024)}, u32[]{:S(2)}) copy-start(f32[1024]{0:T(1024)} %copy-done.112) | copy-start | bytes 12292
  (112 other events, 241.4 us)
Sparse Core Ops, SparseCore 0:
  25.7 22.2 all-reduce.13
  55.6 20.8 all-reduce.15
  99.1 20.8 all-reduce.17
  125.9 20.7 all-reduce.19
  244.3 33.4 all-reduce.21
  299.4 22.3 all-reduce.23
  335.3 20.7 all-reduce.25
  376.8 22.3 all-reduce.27
  406.8 366.2 all-reduce.29
where the time goes:
time: 800 us; the launch traced here: 791 us
  waiting for transfers between devices  398 us (50%)
  matrix products  110 us (14%)
  local copies, waits for them, and re-layouts  108 us (14%)
  blocking collectives  80.8 us (10%)
  other arithmetic  63 us (8%)
  between operations  16 us (2%)
  starting transfers between devices  15.3 us (2%)
    psum x1, waiting for transfers between devices, local(): summed = lax.psum(stacked + (grad_gate,), 'dp')  283 us
    psum x1, blocking collectives, local(): summed = lax.psum(stacked + (grad_gate,), 'dp')  80.8 us
    unnamed x275, local copies, waits for them, and re-layouts  44.4 us
    psum x2, waiting for transfers between devices, layer_backward(): lax.psum(jnp.einsum('rtf,df->rtd', grad_pre, w_up, preferred_element_type...  42.5 us
    psum x4, waiting for transfers between devices, across_cores(): return lax.psum(values, 'mp')  41.9 us
    gather x1, local copies, waits for them, and re-layouts, fetch_neighbours(): fetched[flat_owner, slot_rank]  37 us
    gather x1, local copies, waits for them, and re-layouts, fetch_neighbours(): jnp.take(table, lax.all_to_all(requests, 'dp', split_axis=0, concat_axis=...  17.3 us
    dot_general x4, matrix products, attend_values(): jnp.einsum('rhqk,rkhd->rqhd', probs_low, value_rows, preferred_element_ty...  16.4 us
  transfers between devices with their start and end apart: 11, of which 9 were waited for; matrix products, arithmetic and copies ran while one was open for 13% of the time, Pallas kernels for 0%

commit v1 on v0

--- a/solution.py
+++ b/solution.py
@@ -74,8 +74,73 @@
     return flat_heads(head_mixed).astype(jnp.bfloat16)
 
 
+def other_core(values):
+    return lax.ppermute(values, "mp", [(0, 1), (1, 0)])
+
+
 def across_cores(values):
-    return lax.psum(values, "mp")
+    return values + other_core(values)
+
+
+def partner(values, bit):
+    size = lax.axis_size("dp")
+    return lax.ppermute(values, "dp", [(i, i ^ (1 << bit)) for i in range(size)])
+
+
+def add_low(left, right):
+    return (left.astype(jnp.float32) + right.astype(jnp.float32)).astype(jnp.bfloat16)
+
+
+def scatter_sum(pieces, order):
+    me = lax.axis_index("dp")
+    for bit in order:
+        half = pieces.shape[0] // 2
+        mine = (me >> bit) & 1
+        shape = (half,) + pieces.shape[1:]
+        sent = lax.dynamic_slice(pieces, ((1 - mine) * half, 0, 0), shape)
+        kept = lax.dynamic_slice(pieces, (mine * half, 0, 0), shape)
+        pieces = add_low(kept, partner(sent, bit))
+    return pieces
+
+
+def gather_all(pieces, order):
+    me = lax.axis_index("dp")
+    for bit in reversed(order):
+        mine = (me >> bit) & 1
+        other = partner(pieces, bit)
+        pieces = jnp.concatenate(
+            [jnp.where(mine == 0, pieces, other), jnp.where(mine == 0, other, pieces)], axis=0
+        )
+    return pieces
+
+
+def sum_rows(values, turned):
+    size = lax.axis_size("dp")
+    bits = size.bit_length() - 1
+    order = list(range(bits))
+    if turned:
+        order[0], order[1] = order[1], order[0]
+    pieces = values.astype(jnp.bfloat16).reshape(size, values.shape[0] // size, values.shape[1])
+    return gather_all(scatter_sum(pieces, order), order).reshape(values.shape)
+
+
+def sum_small(values):
+    for bit in range(lax.axis_size("dp").bit_length() - 1):
+        values = values + partner(values, bit)
+    return values
+
+
+def sum_level(grads):
+    gain_attn, wq, wk, wv, wout, gain_ffn, up, down = grads
+    half = wv.shape[0] // 2
+    up = sum_rows(up, False).astype(jnp.float32)
+    down = sum_rows(down, True).astype(jnp.float32)
+    qk = sum_rows(jnp.concatenate([wq, wk], axis=1), False).astype(jnp.float32)
+    vo = jnp.concatenate([jnp.concatenate([wv[:half], wv[half:]], axis=1), wout], axis=0)
+    vo = sum_rows(vo, True).astype(jnp.float32)
+    cols = wq.shape[1]
+    wv = jnp.concatenate([vo[:half, :cols], vo[:half, cols:]], axis=0)
+    return (gain_attn, qk[:, :cols], qk[:, cols:], wv, vo[half:], gain_ffn, up, down)
 
 
 def layer_forward(hidden, memory_rows, allowed, weights):
@@ -111,8 +176,8 @@
     grad_act = jnp.einsum("rtd,fd->rtf", grad_low, w_down, preferred_element_type=jnp.float32)
     grad_pre = gelu_back(grad_act)[0].astype(jnp.bfloat16)
     grad_up = jnp.einsum("rtd,rtf->df", ffn_low, grad_pre, preferred_element_type=jnp.float32)
-    grad_normed = lax.psum(
-        jnp.einsum("rtf,df->rtd", grad_pre, w_up, preferred_element_type=jnp.float32), "mp"
+    grad_normed = across_cores(
+        jnp.einsum("rtf,df->rtd", grad_pre, w_up, preferred_element_type=jnp.float32)
     )
     grad_middle_norm, grad_gain_ffn = ffn_norm_back(grad_normed)
     grad_middle = grad_out + grad_middle_norm
@@ -164,7 +229,7 @@
     ) + jnp.einsum("rte,de->rtd", grad_value, w_value, preferred_element_type=jnp.float32)
     from_query = jnp.einsum("rte,de->rtd", grad_query, w_query, preferred_element_type=jnp.float32)
     from_query = jnp.concatenate([jnp.zeros_like(from_keys[:, :MEM]), from_query], axis=1)
-    grad_normed_attn = lax.psum(from_keys + from_query, "mp")
+    grad_normed_attn = across_cores(from_keys + from_query)
     grad_full, grad_gain_attn = attn_norm_back(grad_normed_attn)
     grad_hidden = grad_middle + grad_full[:, MEM:]
     level_grads = (
@@ -266,11 +331,12 @@
             weights,
         )
         memory_grads[layer_index] = grad_memory
-        per_level[layer_index] = level_grads
+        per_level[layer_index] = sum_level(level_grads)
     stacked = tuple((jnp.stack(grad_parts) for grad_parts in zip(*per_level)))
-    summed = lax.psum(stacked + (grad_gate,), "dp")
-    stacked = summed[:-1]
-    gate_total = summed[-1]
+    small = jnp.concatenate([stacked[0], stacked[5], grad_gate[None]], axis=0)
+    small = sum_small(small)
+    gate_total = small[2 * LAYERS]
+    stacked = (small[:LAYERS],) + stacked[1:5] + (small[LAYERS : 2 * LAYERS],) + stacked[6:]
     return (
         final_rows,
         grad_rows,

time: 800 us -> 526 us (0.66)
  waiting for transfers between devices: 398 us -> 124 us
  starting transfers between devices: 15.3 us -> 119 us
  blocking collectives: 80.8 us -> 0 us
  matrix products: 110 us -> 56.7 us
  other arithmetic: 63 us -> 84.6 us
  local copies, waits for them, and re-layouts: 108 us -> 128 us
  between operations: 16 us -> 4.1 us
    psum x9 -> x0, waiting for transfers between devices: 384 us -> none  [the longest x1 283 us: local(): summed = lax.psum(stacked + (grad_gate,), 'dp')]
    ppermute x0 -> x76, starting transfers between devices: none -> 104 us  [the longest x68 103 us: partner(): return lax.ppermute(values, 'dp', [(i, i ^ 1 << bit) for i in range(size)])]
    psum x1 -> x0, blocking collectives: 80.8 us -> none  [local(): summed = lax.psum(stacked + (grad_gate,), 'dp')]
    ppermute x0 -> x76, waiting for transfers between devices: none -> 78.6 us  [the longest x68 78.2 us: partner(): return lax.ppermute(values, 'dp', [(i, i ^ 1 << bit) for i in range(size)])]
    all_to_all x1, waiting for transfers between devices: 13.5 us -> 45 us  [fetch_neighbours(): lax.all_to_all(jnp.take(table, lax.all_to_all(requests, 'dp', split_axis=...]
    dot_general x4 -> x0, matrix products: 29.5 us -> none  [the longest x2 15.8 us: retrieve(): jnp.einsum('...td,...tkd->...tk', top_rows, neighbours, precision=lax.Pre...]
    unnamed x5 -> x9, other arithmetic: 0.2 us -> 14.9 us
    unnamed x275 -> x320, local copies, waits for them, and re-layouts: 44.4 us -> 45.6 us
  transfers between devices with their start and end apart: 11 -> 78, of which waited for: 9 -> 39; matrix products, arithmetic and copies ran while one was open for 13% -> 30% of each run, Pallas kernels for 0% -> 0%
where the time goes in v1:
time: 526 us; the launch traced here: 516 us
  local copies, waits for them, and re-layouts  128 us (24%)
  waiting for transfers between devices  124 us (24%)
  starting transfers between devices  119 us (23%)
  other arithmetic  84.6 us (16%)
  matrix products  56.7 us (11%)
    ppermute x68, starting transfers between devices, partner(): return lax.ppermute(values, 'dp', [(i, i ^ 1 << bit) for i in range(size)])  103 us
    ppermute x68, waiting for transfers between devices, partner(): return lax.ppermute(values, 'dp', [(i, i ^ 1 << bit) for i in range(size)])  78.2 us
    unnamed x320, local copies, waits for them, and re-layouts  45.6 us
    all_to_all x1, waiting for transfers between devices, fetch_neighbours(): lax.all_to_all(jnp.take(table, lax.all_to_all(requests, 'dp', split_axis=...  45 us
    gather x1, local copies, waits for them, and re-layouts, fetch_neighbours(): fetched[flat_owner, slot_rank]  37.1 us
    gather x1, local copies, waits for them, and re-layouts, fetch_neighbours(): jnp.take(table, lax.all_to_all(requests, 'dp', split_axis=0, concat_axis=...  17.3 us
    unnamed x9, other arithmetic  14.9 us
  transfers between devices with their start and end apart: 78, of which 39 were waited for; matrix products, arithmetic and copies ran while one was open for 30% of the time, Pallas kernels for 0%

profile of v1, /device:TPU:0, one launch (start us, length us, event | category | flops | bytes accessed | tf_op | source)
XLA Modules:
  0.0 516.3 jit_solution(17732459566265357842)
XLA Ops:
  20.7 4.5 reduce-window.6
  26.7 8.6 %scatter_custom_fusion = s32[4096]{0:T(1024)} fusion(s32[2048]{0:T(1024)S(1)} %broadcast_select_fusion.65, s32[2048]{0:T(1024)S(1)} %reshape.1922, s32[]{:T(128)} %constant.39.clone.1), kind=kCustom, calls=%fused_computation.443 | custom fusion | bytes 16388
  35.3 8.1 %all-to-all-start = ((s32[16,1,256]{2,1,0:T(1,128)}), s32[16,1,256]{2,1,0:T(1,128)S(1)}, u32[]{:S(2)}, u32[]{:S(2)}) async-start(s32[16,1,256]{2,1,0:T(1,128)} %bitcast.49), calls=%async_computation | async-start | bytes 32768 | tf_op jit(solution)/shard_map/all_to_all | solution.py:260
  53.4 17.3 %gather_fusion = bf16[4096,512]{1,0:T(8,128)(2,1)} fusion(bf16[1024,512]{1,0:T(8,128)(2,1)S(1)} %copy-done, s32[4096]{0:T(1024)S(1)} %broadcast_clamp_fusion), kind=kCustom, calls=%fused_computation | custom fusion | bytes 8404992 | tf_op jit(solution)/shard_map/jit(_take)/gather | solution.py:259
  70.8 4.0 broadcast_select_fusion
  74.7 6.9 %all-to-all-start.1 = ((bf16[16,256,512]{2,1,0:T(8,128)(2,1)}), bf16[16,256,512]{2,1,0:T(8,128)(2,1)}, u32[]{:S(2)}, u32[]{:S(2)}) async-start(bf16[16,256,512]{2,1,0:T(8,128)(2,1)} %broadcast_select_fusion), calls=%async_computation.1 | async-start | bytes 8388608 | tf_op jit(solution)/shard_map/all_to_all | solution.py:258
  102.3 3.4 convolution_bitcast_fusion.6
  117.9 45.0 %all-to-all-done.1 = bf16[16,256,512]{2,1,0:T(8,128)(2,1)} async-done(((bf16[16,256,512]{2,1,0:T(8,128)(2,1)}), bf16[16,256,512]{2,1,0:T(8,128)(2,1)}, u32[]{:S(2)}, u32[]{:S(2)}) %all-to-all-start.1) | async-done | bytes 4194336 | tf_op jit(solution)/shard_map/all_to_all | solution.py:258
  162.9 37.1 %gather_fusion.1 = bf16[2048,512]{1,0:T(8,128)(2,1)} fusion(bf16[16,256,512]{2,1,0:T(8,128)(2,1)} %all-to-all-done.1, s32[2048]{0:T(1024)S(1)} %bitcast.371), kind=kCustom, calls=%fused_computation.1 | custom fusion | bytes 4210688 | tf_op jit(solution)/shard_map/gather | solution.py:267
  199.9 4.0 reshape.1879
  203.9 6.2 %fusion.5 = (f32[512,4]{1,0:T(8,128)}, f32[512,4]{1,0:T(8,128)}) fusion(f32[512,512]{1,0:T(8,128)} %copy.133, bf16[512,4,512]{2,1,0:T(4,128)(2,1)} %reshape.1879, f32[512,512]{1,0:T(8,128)} %copy.131), kind=kLoop, calls=%fused_computation.24 | loop fusion | flops 5238784 | bytes 4210688
  214.1 8.5 %fusion.7 = (f32[512,512]{1,0:T(8,128)}, f32[512,512]{1,0:T(8,128)}) fusion(bf16[512,4,512]{2,1,0:T(4,128)(2,1)} %reshape.1879, f32[512,4]{1,0:T(8,128)} %copy.134, f32[512,4]{1,0:T(8,128)} %copy.132), kind=kLoop, calls=%fused_computation.26 | loop fusion | flops 4718592 | bytes 4210688
  227.6 3.1 fusion.48
  230.8 3.3 fusion.23
  236.3 6.4 %collective-permute-start.68 = (bf16[8,64,512]{2,1,0:T(8,128)(2,1)}, bf16[8,64,512]{2,1,0:T(8,128)(2,1)}, u32[]{:S(2)}, u32[]{:S(2)}) collective-permute-start(bf16[8,64,512]{2,1,0:T(8,128)(2,1)} %constant_dynamic-slice_fusion.3), channel_id=1, source_target_pairs={{0,4},{2,6},{4,0},{6,2},{8,12},{10,14},{12,8},{14,10},{16,20},{18,... | collective-permute-start | bytes 1572872 | tf_op jit(solution)/shard_map/ppermute | solution.py:87
  260.9 2.9 collective-permute-done.69
  263.9 11.9 %collective-permute-start.70 = (bf16[2,64,512]{2,1,0:T(8,128)(2,1)S(1)}, bf16[2,64,512]{2,1,0:T(8,128)(2,1)S(1)}, u32[]{:S(2)}, u32[]{:S(2)}) collective-permute-start(bf16[2,64,512]{2,1,0:T(8,128)(2,1)S(1)} %constant_dynamic-slice_fusion.1), channel_id=1, source_target_pairs={{0,8},{2,10},{4,12},{6,14},{8,0},{10,2},{12,4},{14,6},{16,24},{18,... | collective-permute-start | bytes 393224 | tf_op jit(solution)/shard_map/ppermute | solution.py:87
  275.9 3.4 collective-permute-start.54
  285.5 2.7 collective-permute-start.72
  317.6 3.4 collective-permute-done.73
  327.1 4.4 collective-permute-done.37
  356.8 3.5 collective-permute-done.42
  362.9 4.0 collective-permute-done.43
  382.0 6.3 %collective-permute-done.60 = bf16[8,64,512]{2,1,0:T(8,128)(2,1)S(1)} collective-permute-done((bf16[8,64,512]{2,1,0:T(8,128)(2,1)S(1)}, bf16[8,64,512]{2,1,0:T(8,128)(2,1)S(1)}, u32[]{:S(2)}, u32[]{:S(2)}) %collective-permute-start.60) | collective-permute-done | bytes 524320 | tf_op jit(solution)/shard_map/ppermute | solution.py:87
  389.3 3.2 collective-permute-done.44
  395.7 3.4 collective-permute-done.45
  439.2 2.8 collective-permute-done.65
  448.6 3.3 collective-permute-done.29
  476.3 3.4 collective-permute-done.34
  497.7 2.8 fusion.153
  505.3 2.8 collective-permute-done.10
  510.4 3.0 copy.99
  (755 shorter events, 278.8 us)
Async XLA Ops:
  19.5 27.1 %collective-permute-start = (f32[1,512,512]{1,2,0:T(8,128)S(1)}, f32[1,512,512]{1,2,0:T(8,128)}, u32[]{:S(2)}, u32[]{:S(2)}) collective-permute-start(f32[1,512,512]{1,2,0:T(8,128)S(1)} %convolution_bitcast_fusion.3), channel_id=1, source_target_pairs={{0,1},{1,0},{2,3},{3,2},{4,5},{5,4},{6,7},{7,6},{8,9},{9,8},{10,11... | collective-permute-start | bytes 3145736 | tf_op jit(solution)/shard_map/ppermute | solution.py:78
  35.3 18.1 %all-to-all-start = ((s32[16,1,256]{2,1,0:T(1,128)}), s32[16,1,256]{2,1,0:T(1,128)S(1)}, u32[]{:S(2)}, u32[]{:S(2)}) async-start(s32[16,1,256]{2,1,0:T(1,128)} %bitcast.49), calls=%async_computation | async-start | bytes 32768 | tf_op jit(solution)/shard_map/all_to_all | solution.py:260
  53.2 28.4 %collective-permute-start.1 = (f32[1,512,512]{1,2,0:T(8,128)}, f32[1,512,512]{1,2,0:T(8,128)}, u32[]{:S(2)}, u32[]{:S(2)}) collective-permute-start(f32[1,512,512]{1,2,0:T(8,128)} %convolution_bitcast_fusion.7), channel_id=1, source_target_pairs={{0,1},{1,0},{2,3},{3,2},{4,5},{5,4},{6,7},{7,6},{8,9},{9,8},{10,11... | collective-permute-start | bytes 3145736 | tf_op jit(solution)/shard_map/ppermute | solution.py:78
  74.7 88.2 %all-to-all-start.1 = ((bf16[16,256,512]{2,1,0:T(8,128)(2,1)}), bf16[16,256,512]{2,1,0:T(8,128)(2,1)}, u32[]{:S(2)}, u32[]{:S(2)}) async-start(bf16[16,256,512]{2,1,0:T(8,128)(2,1)} %broadcast_select_fusion), calls=%async_computation.1 | async-start | bytes 8388608 | tf_op jit(solution)/shard_map/all_to_all | solution.py:258
  236.3 17.5 %collective-permute-start.68 = (bf16[8,64,512]{2,1,0:T(8,128)(2,1)}, bf16[8,64,512]{2,1,0:T(8,128)(2,1)}, u32[]{:S(2)}, u32[]{:S(2)}) collective-permute-start(bf16[8,64,512]{2,1,0:T(8,128)(2,1)} %constant_dynamic-slice_fusion.3), channel_id=1, source_target_pairs={{0,4},{2,6},{4,0},{6,2},{8,12},{10,14},{12,8},{14,10},{16,20},{18,... | collective-permute-start | bytes 1572872 | tf_op jit(solution)/shard_map/ppermute | solution.py:87
  245.4 14.2 %collective-permute-start.52 = (bf16[8,32,1024]{2,1,0:T(8,128)(2,1)}, bf16[8,32,1024]{2,1,0:T(8,128)(2,1)}, u32[]{:S(2)}, u32[]{:S(2)}) collective-permute-start(bf16[8,32,1024]{2,1,0:T(8,128)(2,1)} %constant_dynamic-slice_fusion.11), channel_id=1, source_target_pairs={{0,2},{2,0},{4,6},{6,4},{8,10},{10,8},{12,14},{14,12},{16,18},{18,... | collective-permute-start | bytes 1572872 | tf_op jit(solution)/shard_map/ppermute | solution.py:87
  252.4 37.7 %collective-permute-start.4 = (f32[1,512,512]{1,2,0:T(8,128)S(1)}, f32[1,512,512]{1,2,0:T(8,128)S(1)}, u32[]{:S(2)}, u32[]{:S(2)}) collective-permute-start(f32[1,512,512]{1,2,0:T(8,128)S(1)} %convolution_bitcast_fusion.5), channel_id=1, source_target_pairs={{0,1},{1,0},{2,3},{3,2},{4,5},{5,4},{6,7},{7,6},{8,9},{9,8},{10,11... | collective-permute-start | bytes 3145736 | tf_op jit(solution)/shard_map/ppermute | solution.py:78
  255.0 8.8 %collective-permute-start.69 = (bf16[4,64,512]{2,1,0:T(8,128)(2,1)S(1)}, bf16[4,64,512]{2,1,0:T(8,128)(2,1)S(1)}, u32[]{:S(2)}, u32[]{:S(2)}) collective-permute-start(bf16[4,64,512]{2,1,0:T(8,128)(2,1)S(1)} %constant_dynamic-slice_fusion.2), channel_id=1, source_target_pairs={{0,2},{2,0},{4,6},{6,4},{8,10},{10,8},{12,14},{14,12},{16,18},{18,... | collective-permute-start | bytes 786440 | tf_op jit(solution)/shard_map/ppermute | solution.py:87
  260.9 14.9 %collective-permute-start.53 = (bf16[4,32,1024]{2,1,0:T(8,128)(2,1)S(1)}, bf16[4,32,1024]{2,1,0:T(8,128)(2,1)S(1)}, u32[]{:S(2)}, u32[]{:S(2)}) collective-permute-start(bf16[4,32,1024]{2,1,0:T(8,128)(2,1)S(1)} %constant_dynamic-slice_fusion.10), channel_id=1, source_target_pairs={{0,4},{2,6},{4,0},{6,2},{8,12},{10,14},{12,8},{14,10},{16,20},{18,... | collective-permute-start | bytes 786440 | tf_op jit(solution)/shard_map/ppermute | solution.py:87
  263.9 16.0 %collective-permute-start.70 = (bf16[2,64,512]{2,1,0:T(8,128)(2,1)S(1)}, bf16[2,64,512]{2,1,0:T(8,128)(2,1)S(1)}, u32[]{:S(2)}, u32[]{:S(2)}) collective-permute-start(bf16[2,64,512]{2,1,0:T(8,128)(2,1)S(1)} %constant_dynamic-slice_fusion.1), channel_id=1, source_target_pairs={{0,8},{2,10},{4,12},{6,14},{8,0},{10,2},{12,4},{14,6},{16,24},{18,... | collective-permute-start | bytes 393224 | tf_op jit(solution)/shard_map/ppermute | solution.py:87
  285.5 28.0 %collective-permute-start.72 = (bf16[1,64,512]{2,1,0:T(8,128)(2,1)S(1)}, bf16[1,64,512]{2,1,0:T(8,128)(2,1)}, u32[]{:S(2)}, u32[]{:S(2)}) collective-permute-start(bf16[1,64,512]{2,1,0:T(8,128)(2,1)S(1)} %add_convert_fusion.20), channel_id=1, source_target_pairs={{0,16},{2,18},{4,20},{6,22},{8,24},{10,26},{12,28},{14,30},{16,0},... | collective-permute-start | bytes 196616 | tf_op jit(solution)/shard_map/ppermute | solution.py:87
  288.4 28.1 %collective-permute-start.56 = (bf16[1,32,1024]{2,1,0:T(8,128)(2,1)S(1)}, bf16[1,32,1024]{2,1,0:T(8,128)(2,1)}, u32[]{:S(2)}, u32[]{:S(2)}) collective-permute-start(bf16[1,32,1024]{2,1,0:T(8,128)(2,1)S(1)} %add_convert_fusion.22), channel_id=1, source_target_pairs={{0,16},{2,18},{4,20},{6,22},{8,24},{10,26},{12,28},{14,30},{16,0},... | collective-permute-start | bytes 196616 | tf_op jit(solution)/shard_map/ppermute | solution.py:87
  306.8 18.4 %collective-permute-start.36 = (bf16[8,32,512]{2,1,0:T(8,128)(2,1)S(1)}, bf16[8,32,512]{2,1,0:T(8,128)(2,1)S(1)}, u32[]{:S(2)}, u32[]{:S(2)}) collective-permute-start(bf16[8,32,512]{2,1,0:T(8,128)(2,1)S(1)} %constant_dynamic-slice_fusion.19), channel_id=1, source_target_pairs={{0,4},{2,6},{4,0},{6,2},{8,12},{10,14},{12,8},{14,10},{16,20},{18,... | collective-permute-start | bytes 786440 | tf_op jit(solution)/shard_map/ppermute | solution.py:87
  309.9 17.0 %collective-permute-start.20 = (bf16[8,32,512]{2,1,0:T(8,128)(2,1)S(1)}, bf16[8,32,512]{2,1,0:T(8,128)(2,1)S(1)}, u32[]{:S(2)}, u32[]{:S(2)}) collective-permute-start(bf16[8,32,512]{2,1,0:T(8,128)(2,1)S(1)} %fusion.89), channel_id=1, source_target_pairs={{0,2},{2,0},{4,6},{6,4},{8,10},{10,8},{12,14},{14,12},{16,18},{18,... | collective-permute-start | bytes 786440 | tf_op jit(solution)/shard_map/ppermute | solution.py:87
  313.5 56.5 %collective-permute-start.5 = (f32[1,1024,512]{1,2,0:T(8,128)S(1)}, f32[1,1024,512]{1,2,0:T(8,128)S(1)}, u32[]{:S(2)}, u32[]{:S(2)}) collective-permute-start(f32[1,1024,512]{1,2,0:T(8,128)S(1)} %bitcast_add_fusion.1), channel_id=1, source_target_pairs={{0,1},{1,0},{2,3},{3,2},{4,5},{5,4},{6,7},{7,6},{8,9},{9,8},{10,11... | collective-permute-start | bytes 6291464 | tf_op jit(solution)/shard_map/ppermute | solution.py:78
  321.0 15.1 %collective-permute-start.74 = (bf16[4,64,512]{2,1,0:T(8,128)(2,1)S(1)}, bf16[4,64,512]{2,1,0:T(8,128)(2,1)S(1)}, u32[]{:S(2)}, u32[]{:S(2)}) collective-permute-start(bf16[4,64,512]{2,1,0:T(8,128)(2,1)S(1)} %pad_maximum_fusion.26), channel_id=1, source_target_pairs={{0,2},{2,0},{4,6},{6,4},{8,10},{10,8},{12,14},{14,12},{16,18},{18,... | collective-permute-start | bytes 786440 | tf_op jit(solution)/shard_map/ppermute | solution.py:87
  323.5 14.5 %collective-permute-start.58 = (bf16[4,32,1024]{2,1,0:T(8,128)(2,1)S(1)}, bf16[4,32,1024]{2,1,0:T(8,128)(2,1)S(1)}, u32[]{:S(2)}, u32[]{:S(2)}) collective-permute-start(bf16[4,32,1024]{2,1,0:T(8,128)(2,1)S(1)} %pad_maximum_fusion.24), channel_id=1, source_target_pairs={{0,4},{2,6},{4,0},{6,2},{8,12},{10,14},{12,8},{14,10},{16,20},{18,... | collective-permute-start | bytes 786440 | tf_op jit(solution)/shard_map/ppermute | solution.py:87
  331.6 8.0 %collective-permute-start.38 = (bf16[2,32,512]{2,1,0:T(8,128)(2,1)S(1)}, bf16[2,32,512]{2,1,0:T(8,128)(2,1)S(1)}, u32[]{:S(2)}, u32[]{:S(2)}) collective-permute-start(bf16[2,32,512]{2,1,0:T(8,128)(2,1)S(1)} %constant_dynamic-slice_fusion.17), channel_id=1, source_target_pairs={{0,8},{2,10},{4,12},{6,14},{8,0},{10,2},{12,4},{14,6},{16,24},{18,... | collective-permute-start | bytes 196616 | tf_op jit(solution)/shard_map/ppermute | solution.py:87
  336.2 25.3 %collective-permute-start.75 = (bf16[8,64,512]{2,1,0:T(8,128)(2,1)S(1)}, bf16[8,64,512]{2,1,0:T(8,128)(2,1)S(1)}, u32[]{:S(2)}, u32[]{:S(2)}) collective-permute-start(bf16[8,64,512]{2,1,0:T(8,128)(2,1)S(1)} %pad_maximum_fusion.18), channel_id=1, source_target_pairs={{0,4},{2,6},{4,0},{6,2},{8,12},{10,14},{12,8},{14,10},{16,20},{18,... | collective-permute-start | bytes 1572872 | tf_op jit(solution)/shard_map/ppermute | solution.py:87
  338.1 23.6 %collective-permute-start.59 = (bf16[8,32,1024]{2,1,0:T(8,128)(2,1)S(1)}, bf16[8,32,1024]{2,1,0:T(8,128)(2,1)S(1)}, u32[]{:S(2)}, u32[]{:S(2)}) collective-permute-start(bf16[8,32,1024]{2,1,0:T(8,128)(2,1)S(1)} %pad_maximum_fusion.16), channel_id=1, source_target_pairs={{0,2},{2,0},{4,6},{6,4},{8,10},{10,8},{12,14},{14,12},{16,18},{18,... | collective-permute-start | bytes 1572872 | tf_op jit(solution)/shard_map/ppermute | solution.py:87
  378.3 10.0 %collective-permute-start.60 = (bf16[8,64,512]{2,1,0:T(8,128)(2,1)S(1)}, bf16[8,64,512]{2,1,0:T(8,128)(2,1)S(1)}, u32[]{:S(2)}, u32[]{:S(2)}) collective-permute-start(bf16[8,64,512]{2,1,0:T(8,128)(2,1)S(1)} %constant_dynamic-slice_fusion.7), channel_id=1, source_target_pairs={{0,4},{2,6},{4,0},{6,2},{8,12},{10,14},{12,8},{14,10},{16,20},{18,... | collective-permute-start | bytes 1572872 | tf_op jit(solution)/shard_map/ppermute | solution.py:87
  380.4 12.1 %collective-permute-start.44 = (bf16[8,32,1024]{2,1,0:T(8,128)(2,1)S(1)}, bf16[8,32,1024]{2,1,0:T(8,128)(2,1)S(1)}, u32[]{:S(2)}, u32[]{:S(2)}) collective-permute-start(bf16[8,32,1024]{2,1,0:T(8,128)(2,1)S(1)} %constant_dynamic-slice_fusion.15), channel_id=1, source_target_pairs={{0,2},{2,0},{4,6},{6,4},{8,10},{10,8},{12,14},{14,12},{16,18},{18,... | collective-permute-start | bytes 1572872 | tf_op jit(solution)/shard_map/ppermute | solution.py:87
  381.9 29.8 %collective-permute-start.6 = (f32[1,512,512]{1,2,0:T(8,128)S(1)}, f32[1,512,512]{1,2,0:T(8,128)S(1)}, u32[]{:S(2)}, u32[]{:S(2)}) collective-permute-start(f32[1,512,512]{1,2,0:T(8,128)S(1)} %convolution_bitcast_fusion.4), channel_id=1, source_target_pairs={{0,1},{1,0},{2,3},{3,2},{4,5},{5,4},{6,7},{7,6},{8,9},{9,8},{10,11... | collective-permute-start | bytes 3145736 | tf_op jit(solution)/shard_map/ppermute | solution.py:78
  408.0 26.7 %collective-permute-start.64 = (bf16[1,64,512]{2,1,0:T(8,128)(2,1)S(1)}, bf16[1,64,512]{2,1,0:T(8,128)(2,1)}, u32[]{:S(2)}, u32[]{:S(2)}) collective-permute-start(bf16[1,64,512]{2,1,0:T(8,128)(2,1)S(1)} %add_convert_fusion.21), channel_id=1, source_target_pairs={{0,16},{2,18},{4,20},{6,22},{8,24},{10,26},{12,28},{14,30},{16,0},... | collective-permute-start | bytes 196616 | tf_op jit(solution)/shard_map/ppermute | solution.py:87
  410.4 27.5 %collective-permute-start.48 = (bf16[1,32,1024]{2,1,0:T(8,128)(2,1)S(1)}, bf16[1,32,1024]{2,1,0:T(8,128)(2,1)}, u32[]{:S(2)}, u32[]{:S(2)}) collective-permute-start(bf16[1,32,1024]{2,1,0:T(8,128)(2,1)S(1)} %add_convert_fusion.23), channel_id=1, source_target_pairs={{0,16},{2,18},{4,20},{6,22},{8,24},{10,26},{12,28},{14,30},{16,0},... | collective-permute-start | bytes 196616 | tf_op jit(solution)/shard_map/ppermute | solution.py:87
  429.3 16.5 %collective-permute-start.28 = (bf16[8,32,512]{2,1,0:T(8,128)(2,1)S(1)}, bf16[8,32,512]{2,1,0:T(8,128)(2,1)S(1)}, u32[]{:S(2)}, u32[]{:S(2)}) collective-permute-start(bf16[8,32,512]{2,1,0:T(8,128)(2,1)S(1)} %constant_dynamic-slice_fusion.23), channel_id=1, source_target_pairs={{0,4},{2,6},{4,0},{6,2},{8,12},{10,14},{12,8},{14,10},{16,20},{18,... | collective-permute-start | bytes 786440 | tf_op jit(solution)/shard_map/ppermute | solution.py:87
  432.5 14.8 %collective-permute-start.12 = (bf16[8,32,512]{2,1,0:T(8,128)(2,1)S(1)}, bf16[8,32,512]{2,1,0:T(8,128)(2,1)S(1)}, u32[]{:S(2)}, u32[]{:S(2)}) collective-permute-start(bf16[8,32,512]{2,1,0:T(8,128)(2,1)S(1)} %fusion.91), channel_id=1, source_target_pairs={{0,2},{2,0},{4,6},{6,4},{8,10},{10,8},{12,14},{14,12},{16,18},{18,... | collective-permute-start | bytes 786440 | tf_op jit(solution)/shard_map/ppermute | solution.py:87
  434.7 59.1 %collective-permute-start.7 = (f32[1,1024,512]{1,2,0:T(8,128)S(1)}, f32[1,1024,512]{1,2,0:T(8,128)S(1)}, u32[]{:S(2)}, u32[]{:S(2)}) collective-permute-start(f32[1,1024,512]{1,2,0:T(8,128)S(1)} %bitcast_add_fusion), channel_id=1, source_target_pairs={{0,1},{1,0},{2,3},{3,2},{4,5},{5,4},{6,7},{7,6},{8,9},{9,8},{10,11... | collective-permute-start | bytes 6291464 | tf_op jit(solution)/shard_map/ppermute | solution.py:78
  442.0 14.5 %collective-permute-start.66 = (bf16[4,64,512]{2,1,0:T(8,128)(2,1)S(1)}, bf16[4,64,512]{2,1,0:T(8,128)(2,1)S(1)}, u32[]{:S(2)}, u32[]{:S(2)}) collective-permute-start(bf16[4,64,512]{2,1,0:T(8,128)(2,1)S(1)} %pad_maximum_fusion.25), channel_id=1, source_target_pairs={{0,2},{2,0},{4,6},{6,4},{8,10},{10,8},{12,14},{14,12},{16,18},{18,... | collective-permute-start | bytes 786440 | tf_op jit(solution)/shard_map/ppermute | solution.py:87
  444.5 13.5 %collective-permute-start.50 = (bf16[4,32,1024]{2,1,0:T(8,128)(2,1)S(1)}, bf16[4,32,1024]{2,1,0:T(8,128)(2,1)S(1)}, u32[]{:S(2)}, u32[]{:S(2)}) collective-permute-start(bf16[4,32,1024]{2,1,0:T(8,128)(2,1)S(1)} %pad_maximum_fusion.23), channel_id=1, source_target_pairs={{0,4},{2,6},{4,0},{6,2},{8,12},{10,14},{12,8},{14,10},{16,20},{18,... | collective-permute-start | bytes 786440 | tf_op jit(solution)/shard_map/ppermute | solution.py:87
  456.6 28.6 %collective-permute-start.67 = (bf16[8,64,512]{2,1,0:T(8,128)(2,1)S(1)}, bf16[8,64,512]{2,1,0:T(8,128)(2,1)S(1)}, u32[]{:S(2)}, u32[]{:S(2)}) collective-permute-start(bf16[8,64,512]{2,1,0:T(8,128)(2,1)S(1)} %pad_maximum_fusion.17), channel_id=1, source_target_pairs={{0,4},{2,6},{4,0},{6,2},{8,12},{10,14},{12,8},{14,10},{16,20},{18,... | collective-permute-start | bytes 1572872 | tf_op jit(solution)/shard_map/ppermute | solution.py:87
  458.1 24.7 %collective-permute-start.51 = (bf16[8,32,1024]{2,1,0:T(8,128)(2,1)S(1)}, bf16[8,32,1024]{2,1,0:T(8,128)(2,1)S(1)}, u32[]{:S(2)}, u32[]{:S(2)}) collective-permute-start(bf16[8,32,1024]{2,1,0:T(8,128)(2,1)S(1)} %pad_maximum_fusion.15), channel_id=1, source_target_pairs={{0,2},{2,0},{4,6},{6,4},{8,10},{10,8},{12,14},{14,12},{16,18},{18,... | collective-permute-start | bytes 1572872 | tf_op jit(solution)/shard_map/ppermute | solution.py:87
  (199 other events, 1646.2 us)
